TPU v7x, 32 devices: a whole 2x2x4 slice. The times are simulated.
32 devices in a mesh: expert: 16 (over z, x, core), dp: 2 (over y).
Axes of the slice: x: 2, y: 2, z: 4, core: 2. Of those that a mesh axis runs over, the one named last changes fastest.
Arguments:
- tokens: bfloat16 [64, 2048], P('dp'), may hold values from -6 to 6
- w_gate: bfloat16 [32, 768, 2048], P('expert', 'dp'), may hold values from -2 to 2
- w_up: bfloat16 [32, 768, 2048], P('expert', 'dp'), may hold values from -2 to 2
- w_down: bfloat16 [32, 768, 2048], P('expert', 'dp'), may hold values from -2 to 2
Outputs:
- cosine: float32 [64, 32, 32], P('expert')
All inputs are finite; a program needn't handle non-finite values.
Results may differ from a plain program's by a relative error of at most 0.0014.
Values may be sent and summed in bfloat16 or wider, within the bound.
A program may use at most 64 MiB of HBM per device.

v0:
```python
import jax
import jax.numpy as jnp
from jax import lax
from jax.sharding import PartitionSpec as P


def shards(tokens, w_gate, w_up, w_down):
    block_rows = lax.all_gather(tokens, "dp", axis=0, tiled=True)
    gate = jnp.einsum("td,ehd->teh", block_rows, w_gate, preferred_element_type=jnp.float32)
    upward = jnp.einsum("td,ehd->teh", block_rows, w_up, preferred_element_type=jnp.float32)
    hidden = (jax.nn.silu(gate) * upward).astype(jnp.bfloat16)
    partial_out = jnp.einsum("teh,ehf->etf", hidden, w_down, preferred_element_type=jnp.float32)
    regrouped = lax.all_to_all(partial_out, "expert", split_axis=1, concat_axis=0, tiled=True)
    summed = lax.psum_scatter(regrouped, "dp", scatter_dimension=2, tiled=True)
    features = summed.astype(jnp.bfloat16)
    partial_gram = jnp.einsum(
        "etf,gtf->teg", features, features, preferred_element_type=jnp.float32
    )
    gram = lax.psum(partial_gram, "dp")
    diagonal = jnp.diagonal(gram, axis1=1, axis2=2)
    inverse = lax.rsqrt(diagonal + 1e-06)
    return gram * inverse[:, :, None] * inverse[:, None, :]


def solution(mesh):
    placed = (
        P("dp", None),
        P("expert", "dp", None),
        P("expert", "dp", None),
        P("expert", "dp", None),
    )
    return jax.shard_map(
        shards, mesh=mesh, in_specs=placed, out_specs=P("expert", None, None), check_vma=False
    )
```

profile of v0, /device:TPU:0, one launch (start us, length us, event | category | flops | bytes accessed | tf_op | source)
XLA Modules:
  0.0 99.1 jit_solution(10630486615086355632)
XLA Ops:
  6.5 0.0 copy-start
  6.5 0.0 reduce-scatter.2.cloned.1.call-start
  6.5 7.5 %all_gather.3 = bf16[64,2048]{1,0:T(8,128)(2,1)S(1)} all-gather(bf16[32,2048]{1,0:T(8,128)(2,1)} %param.4), channel_id=1, replica_groups=mesh['expert'=16,'dp'=2] {'dp'}, dimensions={0}, use_global_device_ids=true | all-gather | bytes 393216 | tf_op jit(solution)/shard_map/all_gather | solution.py:8
  14.0 3.7 %fusion.4 = f32[64,2,384]{2,0,1:T(8,128)} fusion(bf16[2,384,2048]{2,1,0:T(8,128)(2,1)} %param.5, bf16[64,2048]{1,0:T(8,128)(2,1)S(1)} %all_gather.3), kind=kOutput, calls=%fused_computation.5 | convolution fusion | flops 201326592 | bytes 3604480 | tf_op jit(solution)/shard_map/td,ehd->teh/dot_general | solution.py:9
  17.7 0.0 copy-done
  17.7 4.6 %fusion.1 = f32[2,64,2048]{2,1,0:T(8,128)} fusion(bf16[2,384,2048]{2,1,0:T(8,128)(2,1)S(1)} %copy-done, bf16[2,384,2048]{2,1,0:T(8,128)(2,1)} %param.6, bf16[64,2048]{1,0:T(8,128)(2,1)S(1)} %all_gather.3, f32[64,2,384]{2,0,1:T(8,128)} %fusion.4), kind=kOutput, calls=%fused_computation.3 | convolution fusion | flops 402948096 | bytes 7798784 | tf_op jit(solution)/shard_map/teh,ehf->etf/dot_general | solution.py:12
  22.3 2.0 %copy.9 = f32[2,64,2048]{2,0,1:T(2,128)S(1)} copy(f32[2,64,2048]{2,1,0:T(8,128)} %fusion.1) | data formatting | bytes 2097152 | tf_op jit(solution)/shard_map/teh,ehf->etf/dot_general | solution.py:12
  24.3 30.8 %all_to_all.18 = f32[2,64,2048]{2,0,1:T(2,128)S(1)} all-to-all(f32[2,64,2048]{2,0,1:T(2,128)S(1)} %copy.9), channel_id=1, replica_groups=mesh['expert'=16,'dp'=2] {'expert'}, dimensions={1} | all-to-all | bytes 2097152 | tf_op jit(solution)/shard_map/all_to_all | solution.py:13
  55.1 1.1 %copy.10 = f32[16,2,4,2048]{3,1,0,2:T(2,128)} copy(f32[16,2,4,2048]{3,1,2,0:T(2,128)S(1)} %bitcast.18) | data formatting | bytes 2097152 | tf_op jit(solution)/shard_map/all_to_all | solution.py:13
  56.2 2.9 %all_to_all.16 = f32[32,4,2048]{2,0,1:T(8,128)} reshape(f32[16,2,4,2048]{3,1,0,2:T(2,128)} %copy.10) | data formatting | bytes 2097152 | tf_op jit(solution)/shard_map/all_to_all | solution.py:13
  59.1 0.0 reduce-scatter.2.cloned.1.call-update
  59.2 20.8 %reduce-scatter.2.cloned.1.call-done = f32[32,4,1024]{2,0,1:T(8,128)} async-done(((f32[32,4,2048]{2,0,1:T(8,128)}), f32[32,4,1024]{2,0,1:T(8,128)}) %reduce-scatter.2.cloned.1.call-update) | async-done | bytes 524304 | tf_op jit(solution)/shard_map/reduce_scatter | solution.py:14
  80.0 1.4 %fusion.6 = f32[4,32,32]{2,1,0:T(8,128)S(1)} fusion(f32[32,4,1024]{2,0,1:T(8,128)} %reduce-scatter.2.cloned.1.call-done), kind=kOutput, calls=%fused_computation.7 | convolution fusion | flops 8519680 | bytes 540672 | tf_op jit(solution)/shard_map/etf,gtf->teg/dot_general | solution.py:16
  81.4 7.7 %psum.7 = f32[4,32,32]{2,1,0:T(8,128)S(1)} all-reduce(f32[4,32,32]{2,1,0:T(8,128)S(1)} %fusion.6), channel_id=1, replica_groups=mesh['expert'=16,'dp'=2] {'dp'}, use_global_device_ids=true, to_apply=%region_1.2 | all-reduce | flops 4096 | bytes 32768 | tf_op jit(solution)/shard_map/psum | solution.py:19
  89.0 1.1 %copy.11 = f32[4,32,32]{0,2,1:T(8,128)} copy(f32[4,32,32]{2,1,0:T(8,128)S(1)} %psum.7) | data formatting | bytes 32768 | tf_op jit(solution)/shard_map/psum | solution.py:19
  90.1 1.3 %gather_fusion = f32[32,4]{1,0:T(8,128)S(1)} fusion(f32[4,32,32]{0,2,1:T(8,128)} %copy.11, s32[32]{0:T(128)S(1)} %or_bitcast_fusion), kind=kCustom, calls=%fused_computation | custom fusion | bytes 1280 | tf_op jit(solution)/shard_map/jit(diagonal)/gather | solution.py:20
  91.4 0.1 copy.12
  91.5 0.7 multiply_multiply_fusion
  (2 shorter events, 0.0 us)
Async XLA Ops:
  6.5 11.1 %copy-start = (bf16[2,384,2048]{2,1,0:T(8,128)(2,1)S(1)}, bf16[2,384,2048]{2,1,0:T(8,128)(2,1)}, u32[]{:S(2)}) copy-start(bf16[2,384,2048]{2,1,0:T(8,128)(2,1)} %param.7) | copy-start | bytes 9437188
  6.5 73.4 %reduce-scatter.2.cloned.1.call-start = ((), (), s32[]{:S(2)}) async-start(), calls=%async_computation.2 | async-start | bytes 1572864 | tf_op jit(solution)/shard_map/reduce_scatter | solution.py:14
Sparse Core Ops, SparseCore 0:
  59.3 20.6 reduce-scatter.1
where the time goes:
time: 99.4 us; the launch traced here: 99.1 us
  blocking collectives  45.9 us (46%)
  waiting for transfers between devices  20.8 us (21%)
  between operations  13.4 us (13%)
  matrix products  9.65 us (10%)
  local copies, waits for them, and re-layouts  8.57 us (9%)
    all_to_all x1, blocking collectives, shards(): lax.all_to_all(partial_out, 'expert', split_axis=1, concat_axis=0, tiled=...  30.8 us
    reduce_scatter x1, waiting for transfers between devices, shards(): summed = lax.psum_scatter(regrouped, 'dp', scatter_dimension=2, tiled=True)  20.8 us
    psum x1, blocking collectives, shards(): gram = lax.psum(partial_gram, 'dp')  7.66 us
    all_gather x1, blocking collectives, shards(): block_rows = lax.all_gather(tokens, 'dp', axis=0, tiled=True)  7.47 us
    dot_general x1, matrix products, shards(): jnp.einsum('teh,ehf->etf', hidden, w_down, preferred_element_type=jnp.flo...  4.61 us
    all_to_all x2, local copies, waits for them, and re-layouts, shards(): lax.all_to_all(partial_out, 'expert', split_axis=1, concat_axis=0, tiled=...  4.05 us
    dot_general x1, matrix products, shards(): jnp.einsum('td,ehd->teh', block_rows, w_gate, preferred_element_type=jnp....  3.65 us
    dot_general x1, local copies, waits for them, and re-layouts, shards(): jnp.einsum('teh,ehf->etf', hidden, w_down, preferred_element_type=jnp.flo...  2.03 us
  transfers between devices with their start and end apart: 1, of which 1 were waited for; matrix products, arithmetic and copies ran while one was open for 0% of the time, Pallas kernels for 0%

commit v1 on v0

v1 whole, which is shorter than its diff:
```python
import functools

import jax
import jax.numpy as jnp
from jax import lax
from jax.experimental import pallas as pl
from jax.experimental.pallas import tpu as pltpu
from jax.sharding import PartitionSpec as P

F32 = jnp.float32
BF16 = jnp.bfloat16
MESH = pl.DeviceIdType.MESH


def log2(n):
    assert n & (n - 1) == 0
    return n.bit_length() - 1


def matrix_of(rows, cols, want, keep=None):
    r = lax.broadcasted_iota(jnp.int32, (rows, cols), 0)
    q = lax.broadcasted_iota(jnp.int32, (rows, cols), 1)
    hit = q == want(r)
    if keep is not None:
        hit = hit & keep(r)
    return jnp.where(hit, 1.0, 0.0).astype(BF16)


def kernel(cfg, tok_hbm, wg_hbm, wu_hbm, wd_hbm, out_ref,
           tok, wg, wu, wd, perm_send, perm_recv, own, ysend, yrecv, xsend, xrecv,
           gsend, grecv,
           w_sem, t_sem, ts_sem, tr_sem, ys_sem, yr_sem, xs_sem, xr_sem, gs_sem, gr_sem):
    n_dp, n_ex, T, Tl, D, H, E_loc, ec, G, L, Tk = cfg
    E = n_ex * E_loc
    Fk = D // n_dp
    R = ec * G * Tk
    chunks = E_loc // ec
    dp = lax.axis_index("dp")
    ex = lax.axis_index("expert")

    def dp_peer(s):
        return lax.rem(dp + s, n_dp)

    own_tok = pltpu.make_async_copy(tok_hbm, tok.at[dp], t_sem)
    own_tok.start()
    loads = {}
    for e in range(E_loc):
        for k, (src, dst) in enumerate(((wg_hbm, wg), (wu_hbm, wu), (wd_hbm, wd))):
            loads[e, k] = pltpu.make_async_copy(src.at[e], dst.at[e], w_sem.at[e, k])
            loads[e, k].start()

    barrier = pltpu.get_barrier_semaphore()
    for s in range(1, n_dp):
        pl.semaphore_signal(barrier, inc=1, device_id=(ex, dp_peer(s)), device_id_type=MESH)

    def greet(s, carry):
        pl.semaphore_signal(
            barrier, inc=1, device_id=(lax.rem(ex + s, n_ex), dp), device_id_type=MESH
        )
        return carry

    lax.fori_loop(1, n_ex, greet, 0)
    pl.semaphore_wait(barrier, n_dp - 1 + n_ex - 1)

    tok_copies = []
    for s in range(1, n_dp):
        copy = pltpu.make_async_remote_copy(
            src_ref=tok_hbm, dst_ref=tok.at[dp],
            send_sem=ts_sem.at[s - 1], recv_sem=tr_sem.at[s - 1],
            device_id=(ex, dp_peer(s)), device_id_type=MESH,
        )
        copy.start()
        tok_copies.append(copy)

    GE = ec * G
    rows = GE * T
    lR, lTk = log2(R), log2(Tk)
    perm_send[...] = matrix_of(
        rows, rows,
        lambda r: ((r >> lTk) & (GE - 1)) * T + (r >> lR) * Tk + (r & (Tk - 1)),
    )
    lE, lEl, lec = log2(E), log2(E_loc), log2(ec)

    for c in range(chunks):
        def want(r):
            g = r >> (lTk + lE)
            j = (r >> lE) & (Tk - 1)
            e = r & (E - 1)
            el = e & (ec - 1)
            return (e >> lEl) * R + (el * G + g) * Tk + j

        perm_recv[c] = matrix_of(
            G * Tk * E, n_ex * R, want,
            lambda r: ((r & (E_loc - 1)) >> lec) == c,
        )

    own_tok.wait()
    for copy in tok_copies:
        copy.wait_recv()
    tokens = tok[...].reshape(T, D)

    nt = (((1,), (1,)), ((), ()))
    y_copies = {}
    for e in range(E_loc):
        loads[e, 0].wait()
        gate = lax.dot_general(tokens, wg[e], nt, preferred_element_type=F32)
        loads[e, 1].wait()
        up = lax.dot_general(tokens, wu[e], nt, preferred_element_type=F32)
        hidden = (gate / (1.0 + jnp.exp(-gate)) * up).astype(BF16)
        loads[e, 2].wait()
        for s in range(1, n_dp):
            cols = pl.ds(pl.multiple_of(dp_peer(s) * Fk, Fk), Fk)
            part = jnp.dot(hidden, wd[e, :, cols], preferred_element_type=F32)
            ysend[e, s - 1] = part.astype(BF16)
            copy = pltpu.make_async_remote_copy(
                src_ref=ysend.at[e, s - 1], dst_ref=yrecv.at[e, s - 1],
                send_sem=ys_sem.at[e, s - 1], recv_sem=yr_sem.at[e, s - 1],
                device_id=(ex, dp_peer(s)), device_id_type=MESH,
            )
            copy.start()
            y_copies[e, s] = copy
        cols = pl.ds(pl.multiple_of(dp * Fk, Fk), Fk)
        own[e] = jnp.dot(hidden, wd[e, :, cols], preferred_element_type=F32)

    for c in range(chunks):
        pieces = []
        for e in range(c * ec, (c + 1) * ec):
            total = own[e]
            for s in range(1, n_dp):
                y_copies[e, s].wait_recv()
                total += yrecv[e, s - 1].astype(F32)
            total = total.astype(BF16)
            pieces += [total[:, g * L:(g + 1) * L] for g in range(G)]
        stacked = jnp.concatenate(pieces, axis=0)
        xsend[c] = jnp.dot(
            perm_send[...], stacked, preferred_element_type=F32
        ).astype(BF16)
        mine = pl.ds(pl.multiple_of(ex * R, R), R)

        def send(s, carry):
            to = lax.rem(ex + s, n_ex)
            theirs = pl.ds(pl.multiple_of(to * R, R), R)
            pltpu.make_async_remote_copy(
                src_ref=xsend.at[c, theirs], dst_ref=xrecv.at[c, mine],
                send_sem=xs_sem.at[c], recv_sem=xr_sem.at[c],
                device_id=(to, dp), device_id_type=MESH,
            ).start()
            return carry

        lax.fori_loop(1, n_ex, send, 0, unroll=n_ex <= 16)
        xrecv[c, mine] = xsend[c, mine]

    total = None
    for c in range(chunks):
        most = xrecv.at[c, pl.ds(0, (n_ex - 1) * R)]
        pltpu.make_async_copy(most, most, xr_sem.at[c]).wait()
        term = jnp.dot(perm_recv[c], xrecv[c], preferred_element_type=F32)
        total = term if total is None else total + term
    total = total.astype(BF16)
    per_token = jnp.concatenate(
        [total[g * Tk * E:(g + 1) * Tk * E] for g in range(G)], axis=1
    )
    full = lax.dot_general(per_token, per_token, nt, preferred_element_type=F32)
    lane = lax.broadcasted_iota(jnp.int32, (E, Tk * E), 1)
    row = lax.broadcasted_iota(jnp.int32, (E, Tk * E), 0)
    gram = jnp.zeros((E, Tk * E), F32)
    for j in range(Tk):
        gram = jnp.where((lane >> lE) == j, full[j * E:(j + 1) * E], gram)
    gsend[...] = gram
    g_copies = []
    for s in range(1, n_dp):
        copy = pltpu.make_async_remote_copy(
            src_ref=gsend, dst_ref=grecv.at[s - 1],
            send_sem=gs_sem.at[s - 1], recv_sem=gr_sem.at[s - 1],
            device_id=(ex, dp_peer(s)), device_id_type=MESH,
        )
        copy.start()
        g_copies.append(copy)
    for copy in tok_copies:
        copy.wait_send()
    for copy in y_copies.values():
        copy.wait_send()
    for c in range(chunks):
        most = xsend.at[c, pl.ds(0, (n_ex - 1) * R)]
        pltpu.make_async_copy(most, most, xs_sem.at[c]).wait()
    for s in range(1, n_dp):
        g_copies[s - 1].wait_recv()
        gram += grecv[s - 1]
    diagonal = jnp.where((lane & (E - 1)) == row, gram, 0.0)
    along = lax.rsqrt(jnp.sum(diagonal, axis=0, keepdims=True) + 1e-06)
    for j in range(Tk):
        block = slice(j * E, (j + 1) * E)
        down = lax.rsqrt(jnp.sum(diagonal[:, block], axis=1, keepdims=True) + 1e-06)
        out_ref[j] = gram[:, block] * down * along[:, block]
    for copy in g_copies:
        copy.wait_send()


def shards(n_dp, n_ex, tokens, w_gate, w_up, w_down):
    Tl, D = tokens.shape
    E_loc, H, _ = w_gate.shape
    T = Tl * n_dp
    Tk = T // n_ex
    Fk = D // n_dp
    ec = 1 if Tk * (Fk // 128) >= 16 else E_loc
    G = max(1, 16 // (Tk * ec))
    L = Fk // G
    R = ec * G * Tk
    E = n_ex * E_loc
    chunks = E_loc // ec
    cfg = (n_dp, n_ex, T, Tl, D, H, E_loc, ec, G, L, Tk)
    dma = pltpu.SemaphoreType.DMA
    peers = n_dp - 1
    return pl.pallas_call(
        functools.partial(kernel, cfg),
        out_shape=jax.ShapeDtypeStruct((Tk, E, E), F32),
        in_specs=[pl.BlockSpec(memory_space=pl.ANY)] * 4,
        out_specs=pl.BlockSpec(memory_space=pltpu.VMEM),
        scratch_shapes=[
            pltpu.VMEM((n_dp, Tl, D), BF16),
            pltpu.VMEM((E_loc, H, D), BF16),
            pltpu.VMEM((E_loc, H, D), BF16),
            pltpu.VMEM((E_loc, H, D), BF16),
            pltpu.VMEM((ec * G * T, ec * G * T), BF16),
            pltpu.VMEM((chunks, G * Tk * E, n_ex * R), BF16),
            pltpu.VMEM((E_loc, T, Fk), F32),
            pltpu.VMEM((E_loc, peers, T, Fk), BF16),
            pltpu.VMEM((E_loc, peers, T, Fk), BF16),
            pltpu.VMEM((chunks, n_ex * R, L), BF16),
            pltpu.VMEM((chunks, n_ex * R, L), BF16),
            pltpu.VMEM((E, Tk * E), F32),
            pltpu.VMEM((peers, E, Tk * E), F32),
            dma((E_loc, 3)),
            dma,
            dma((peers,)),
            dma((peers,)),
            dma((E_loc, peers)),
            dma((E_loc, peers)),
            dma((chunks,)),
            dma((chunks,)),
            dma((peers,)),
            dma((peers,)),
        ],
        compiler_params=pltpu.CompilerParams(
            collective_id=0, has_side_effects=True, vmem_limit_bytes=48 * 1024 * 1024
        ),
        cost_estimate=pl.CostEstimate(
            flops=6 * E_loc * T * D * H, bytes_accessed=6 * E_loc * H * D,
            transcendentals=E_loc * T * H,
        ),
    )(tokens, w_gate, w_up, w_down)


def solution(mesh):
    placed = (
        P("dp", None),
        P("expert", "dp", None),
        P("expert", "dp", None),
        P("expert", "dp", None),
    )
    return jax.shard_map(
        functools.partial(shards, mesh.shape["dp"], mesh.shape["expert"]),
        mesh=mesh, in_specs=placed, out_specs=P("expert", None, None), check_vma=False,
    )
```

time: 99.4 us -> 31.8 us (0.32)
  blocking collectives: 45.9 us -> 0 us
  Pallas kernels: 0 us -> 28.2 us
  waiting for transfers between devices: 20.8 us -> 0 us
  between operations: 13.4 us -> 0.01 us
  matrix products: 9.65 us -> 0 us
  local copies, waits for them, and re-layouts: 8.57 us -> 3.42 us
    all_to_all x1 -> x0, blocking collectives: 30.8 us -> none  [shards(): lax.all_to_all(partial_out, 'expert', split_axis=1, concat_axis=0, tiled=...]
    pallas_call x0 -> x1, Pallas kernels: none -> 28.2 us  [shards(): pl.pallas_call(functools.partial(kernel, cfg), out_shape=jax.ShapeDtypeSt...]
    reduce_scatter x1 -> x0, waiting for transfers between devices: 20.8 us -> none  [shards(): summed = lax.psum_scatter(regrouped, 'dp', scatter_dimension=2, tiled=True)]
    dot_general x3 -> x0, matrix products: 9.65 us -> none  [the longest x1 4.61 us: shards(): jnp.einsum('teh,ehf->etf', hidden, w_down, preferred_element_type=jnp.flo...]
    psum x1 -> x0, blocking collectives: 7.66 us -> none  [shards(): gram = lax.psum(partial_gram, 'dp')]
    all_gather x1 -> x0, blocking collectives: 7.47 us -> none  [shards(): block_rows = lax.all_gather(tokens, 'dp', axis=0, tiled=True)]
    all_to_all x2 -> x0, local copies, waits for them, and re-layouts: 4.05 us -> none  [shards(): lax.all_to_all(partial_out, 'expert', split_axis=1, concat_axis=0, tiled=...]
    unnamed x2 -> x5, local copies, waits for them, and re-layouts: 0.01 us -> 3.42 us
  transfers between devices with their start and end apart: 1 -> 0, of which waited for: 1 -> 0; matrix products, arithmetic and copies ran while one was open for 0% -> 0% of each run, Pallas kernels for 0% -> 0%
where the time goes in v1:
time: 31.8 us; the launch traced here: 31.7 us
  Pallas kernels  28.2 us (89%)
  local copies, waits for them, and re-layouts  3.42 us (11%)
    pallas_call x1, Pallas kernels, shards(): pl.pallas_call(functools.partial(kernel, cfg), out_shape=jax.ShapeDtypeSt...  28.2 us
    unnamed x5, local copies, waits for them, and re-layouts  3.42 us

profile of v1, /device:TPU:0, one launch (start us, length us, event | category | flops | bytes accessed | tf_op | source)
XLA Modules:
  0.0 31.7 jit_solution(14730447036299423322)
XLA Ops:
  0.0 0.0 copy-start
  0.0 1.9 %copy-done = bf16[2,384,2048]{2,1,0:T(8,128)(2,1)S(1)} copy-done((bf16[2,384,2048]{2,1,0:T(8,128)(2,1)S(1)}, bf16[2,384,2048]{2,1,0:T(8,128)(2,1)}, u32[]{:S(2)}) %copy-start) | copy-done | bytes 3145752
  1.9 0.0 copy-start.1
  1.9 0.9 %copy-done.1 = bf16[32,2048]{1,0:T(8,128)(2,1)S(1)} copy-done((bf16[32,2048]{1,0:T(8,128)(2,1)S(1)}, bf16[32,2048]{1,0:T(8,128)(2,1)}, u32[]{:S(2)}) %copy-start.1) | copy-done | bytes 131096
  2.8 28.2 %shard_map.46 = f32[4,32,32]{2,1,0:T(8,128)S(1)} custom-call(bf16[32,2048]{1,0:T(8,128)(2,1)S(1)} %copy-done.1, bf16[2,384,2048]{2,1,0:T(8,128)(2,1)S(1)} %copy-done, bf16[2,384,2048]{2,1,0:T(8,128)(2,1)} %wu_hbm.1, bf16[2,384,2048]{2,1,0:T(8,128)(2,1)} %wd_hbm.1), custom_call_target="tpu_custom_call" | custom-call | flops 603979776 | bytes 9437184 | tf_op jit(solution)/shard_map/pallas_call | solution.py:214
  31.0 0.6 %copy.6 = f32[4,32,32]{2,1,0:T(8,128)} copy(f32[4,32,32]{2,1,0:T(8,128)S(1)} %shard_map.46) | data formatting | bytes 32768
Async XLA Ops:
  0.0 1.9 %copy-start = (bf16[2,384,2048]{2,1,0:T(8,128)(2,1)S(1)}, bf16[2,384,2048]{2,1,0:T(8,128)(2,1)}, u32[]{:S(2)}) copy-start(bf16[2,384,2048]{2,1,0:T(8,128)(2,1)} %wg_hbm.1) | copy-start | bytes 9437188
  1.9 0.9 %copy-start.1 = (bf16[32,2048]{1,0:T(8,128)(2,1)S(1)}, bf16[32,2048]{1,0:T(8,128)(2,1)}, u32[]{:S(2)}) copy-start(bf16[32,2048]{1,0:T(8,128)(2,1)} %tok_hbm.1) | copy-start | bytes 393220

commit v2 on v1

--- a/solution.py
+++ b/solution.py
@@ -41,7 +41,19 @@
     def dp_peer(s):
         return lax.rem(dp + s, n_dp)
 
-    own_tok = pltpu.make_async_copy(tok_hbm, tok.at[dp], t_sem)
+    barrier = pltpu.get_barrier_semaphore()
+    for s in range(1, n_dp):
+        pl.semaphore_signal(barrier, inc=1, device_id=(ex, dp_peer(s)), device_id_type=MESH)
+
+    def greet(s, carry):
+        pl.semaphore_signal(
+            barrier, inc=1, device_id=(lax.rem(ex + s, n_ex), dp), device_id_type=MESH
+        )
+        return carry
+
+    lax.fori_loop(1, n_ex, greet, 0)
+
+    own_tok = pltpu.make_async_copy(tok_hbm, tok.at[0], t_sem)
     own_tok.start()
     loads = {}
     for e in range(E_loc):
@@ -49,28 +61,55 @@
             loads[e, k] = pltpu.make_async_copy(src.at[e], dst.at[e], w_sem.at[e, k])
             loads[e, k].start()
 
-    barrier = pltpu.get_barrier_semaphore()
-    for s in range(1, n_dp):
-        pl.semaphore_signal(barrier, inc=1, device_id=(ex, dp_peer(s)), device_id_type=MESH)
-
-    def greet(s, carry):
-        pl.semaphore_signal(
-            barrier, inc=1, device_id=(lax.rem(ex + s, n_ex), dp), device_id_type=MESH
-        )
-        return carry
-
-    lax.fori_loop(1, n_ex, greet, 0)
     pl.semaphore_wait(barrier, n_dp - 1 + n_ex - 1)
 
     tok_copies = []
     for s in range(1, n_dp):
         copy = pltpu.make_async_remote_copy(
-            src_ref=tok_hbm, dst_ref=tok.at[dp],
+            src_ref=tok_hbm, dst_ref=tok.at[s],
             send_sem=ts_sem.at[s - 1], recv_sem=tr_sem.at[s - 1],
             device_id=(ex, dp_peer(s)), device_id_type=MESH,
         )
         copy.start()
         tok_copies.append(copy)
+
+    nt = (((1,), (1,)), ((), ()))
+    y_copies = {}
+
+    def hidden_of(tokens, e):
+        gate = lax.dot_general(tokens, wg[e], nt, preferred_element_type=F32)
+        up = lax.dot_general(tokens, wu[e], nt, preferred_element_type=F32)
+        return (gate / (1.0 + jnp.exp(-gate)) * up).astype(BF16)
+
+    def project_theirs(hidden, e, slots):
+        for s in range(1, n_dp):
+            cols = pl.ds(pl.multiple_of(dp_peer(s) * Fk, Fk), Fk)
+            part = jnp.dot(hidden, wd[e, :, cols], preferred_element_type=F32).astype(BF16)
+            for n, k in enumerate(slots):
+                owner = lax.rem(dp + n_dp - k, n_dp)
+                ysend[e, s - 1, owner] = part[n * Tl:(n + 1) * Tl]
+                copy = pltpu.make_async_remote_copy(
+                    src_ref=ysend.at[e, s - 1, owner], dst_ref=yrecv.at[e, s - 1, owner],
+                    send_sem=ys_sem.at[e, s - 1, k], recv_sem=yr_sem.at[e, s - 1, k],
+                    device_id=(ex, dp_peer(s)), device_id_type=MESH,
+                )
+                copy.start()
+                y_copies[e, s, k] = copy
+
+    def project_mine(hidden, e, slots):
+        cols = pl.ds(pl.multiple_of(dp * Fk, Fk), Fk)
+        part = jnp.dot(hidden, wd[e, :, cols], preferred_element_type=F32)
+        for n, k in enumerate(slots):
+            own[e, lax.rem(dp + n_dp - k, n_dp)] = part[n * Tl:(n + 1) * Tl]
+
+    own_tok.wait()
+    for e in range(E_loc):
+        loads[e, 0].wait()
+        loads[e, 1].wait()
+        hidden = hidden_of(tok[0], e)
+        loads[e, 2].wait()
+        project_theirs(hidden, e, (0,))
+        project_mine(hidden, e, (0,))
 
     GE = ec * G
     rows = GE * T
@@ -94,41 +133,24 @@
             lambda r: ((r & (E_loc - 1)) >> lec) == c,
         )
 
-    own_tok.wait()
     for copy in tok_copies:
         copy.wait_recv()
-    tokens = tok[...].reshape(T, D)
-
-    nt = (((1,), (1,)), ((), ()))
-    y_copies = {}
-    for e in range(E_loc):
-        loads[e, 0].wait()
-        gate = lax.dot_general(tokens, wg[e], nt, preferred_element_type=F32)
-        loads[e, 1].wait()
-        up = lax.dot_general(tokens, wu[e], nt, preferred_element_type=F32)
-        hidden = (gate / (1.0 + jnp.exp(-gate)) * up).astype(BF16)
-        loads[e, 2].wait()
-        for s in range(1, n_dp):
-            cols = pl.ds(pl.multiple_of(dp_peer(s) * Fk, Fk), Fk)
-            part = jnp.dot(hidden, wd[e, :, cols], preferred_element_type=F32)
-            ysend[e, s - 1] = part.astype(BF16)
-            copy = pltpu.make_async_remote_copy(
-                src_ref=ysend.at[e, s - 1], dst_ref=yrecv.at[e, s - 1],
-                send_sem=ys_sem.at[e, s - 1], recv_sem=yr_sem.at[e, s - 1],
-                device_id=(ex, dp_peer(s)), device_id_type=MESH,
-            )
-            copy.start()
-            y_copies[e, s] = copy
-        cols = pl.ds(pl.multiple_of(dp * Fk, Fk), Fk)
-        own[e] = jnp.dot(hidden, wd[e, :, cols], preferred_element_type=F32)
+    if n_dp > 1:
+        hidden = []
+        for e in range(E_loc):
+            hidden.append(hidden_of(tok[1:].reshape(T - Tl, D), e))
+            project_theirs(hidden[e], e, range(1, n_dp))
+        for e in range(E_loc):
+            project_mine(hidden[e], e, range(1, n_dp))
 
     for c in range(chunks):
         pieces = []
         for e in range(c * ec, (c + 1) * ec):
-            total = own[e]
+            total = own[e].reshape(T, Fk)
             for s in range(1, n_dp):
-                y_copies[e, s].wait_recv()
-                total += yrecv[e, s - 1].astype(F32)
+                for k in range(n_dp):
+                    y_copies[e, s, k].wait_recv()
+                total += yrecv[e, s - 1].reshape(T, Fk).astype(F32)
             total = total.astype(BF16)
             pieces += [total[:, g * L:(g + 1) * L] for g in range(G)]
         stacked = jnp.concatenate(pieces, axis=0)
@@ -223,9 +245,9 @@
             pltpu.VMEM((E_loc, H, D), BF16),
             pltpu.VMEM((ec * G * T, ec * G * T), BF16),
             pltpu.VMEM((chunks, G * Tk * E, n_ex * R), BF16),
-            pltpu.VMEM((E_loc, T, Fk), F32),
-            pltpu.VMEM((E_loc, peers, T, Fk), BF16),
-            pltpu.VMEM((E_loc, peers, T, Fk), BF16),
+            pltpu.VMEM((E_loc, n_dp, Tl, Fk), F32),
+            pltpu.VMEM((E_loc, peers, n_dp, Tl, Fk), BF16),
+            pltpu.VMEM((E_loc, peers, n_dp, Tl, Fk), BF16),
             pltpu.VMEM((chunks, n_ex * R, L), BF16),
             pltpu.VMEM((chunks, n_ex * R, L), BF16),
             pltpu.VMEM((E, Tk * E), F32),
@@ -234,15 +256,15 @@
             dma,
             dma((peers,)),
             dma((peers,)),
-            dma((E_loc, peers)),
-            dma((E_loc, peers)),
+            dma((E_loc, peers, n_dp)),
+            dma((E_loc, peers, n_dp)),
             dma((chunks,)),
             dma((chunks,)),
             dma((peers,)),
             dma((peers,)),
         ],
         compiler_params=pltpu.CompilerParams(
-            collective_id=0, has_side_effects=True, vmem_limit_bytes=48 * 1024 * 1024
+            collective_id=0, has_side_effects=True, vmem_limit_bytes=60 * 1024 * 1024
         ),
         cost_estimate=pl.CostEstimate(
             flops=6 * E_loc * T * D * H, bytes_accessed=6 * E_loc * H * D,

time: 31.8 us -> 28.3 us (0.89)
  local copies, waits for them, and re-layouts: 3.42 us -> 1.47 us
  Pallas kernels: 28.2 us -> 26.7 us
    unnamed x5 -> x1, local copies, waits for them, and re-layouts: 3.42 us -> 1.47 us
    pallas_call x1, Pallas kernels: 28.2 us -> 26.7 us  [shards(): pl.pallas_call(functools.partial(kernel, cfg), out_shape=jax.ShapeDtypeSt...]
where the time goes in v2:
time: 28.3 us; the launch traced here: 28.2 us
  Pallas kernels  26.7 us (94%)
  local copies, waits for them, and re-layouts  1.47 us (5%)
    pallas_call x1, Pallas kernels, shards(): pl.pallas_call(functools.partial(kernel, cfg), out_shape=jax.ShapeDtypeSt...  26.7 us
    unnamed x1, local copies, waits for them, and re-layouts  1.47 us

profile of v2, /device:TPU:0, one launch (start us, length us, event | category | flops | bytes accessed | tf_op | source)
XLA Modules:
  0.0 28.2 jit_solution(15791189696341893017)
XLA Ops:
  0.0 26.7 %shard_map.46 = f32[4,32,32]{2,1,0:T(8,128)} custom-call(bf16[32,2048]{1,0:T(8,128)(2,1)} %tok_hbm.1, bf16[2,384,2048]{2,1,0:T(8,128)(2,1)} %wg_hbm.1, bf16[2,384,2048]{2,1,0:T(8,128)(2,1)} %wu_hbm.1, bf16[2,384,2048]{2,1,0:T(8,128)(2,1)} %wd_hbm.1), custom_call_target="tpu_custom_call" | custom-call | flops 603979776 | bytes 9437184 | tf_op jit(solution)/shard_map/pallas_call | solution.py:236
  26.7 1.5 %copy.6 = f32[4,32,32]{2,1,0:T(8,128)} copy(f32[4,32,32]{2,1,0:T(8,128)} %shard_map.46) | data formatting | bytes 32768

commit v3 on v2

--- a/solution.py
+++ b/solution.py
@@ -118,21 +118,6 @@
         rows, rows,
         lambda r: ((r >> lTk) & (GE - 1)) * T + (r >> lR) * Tk + (r & (Tk - 1)),
     )
-    lE, lEl, lec = log2(E), log2(E_loc), log2(ec)
-
-    for c in range(chunks):
-        def want(r):
-            g = r >> (lTk + lE)
-            j = (r >> lE) & (Tk - 1)
-            e = r & (E - 1)
-            el = e & (ec - 1)
-            return (e >> lEl) * R + (el * G + g) * Tk + j
-
-        perm_recv[c] = matrix_of(
-            G * Tk * E, n_ex * R, want,
-            lambda r: ((r & (E_loc - 1)) >> lec) == c,
-        )
-
     for copy in tok_copies:
         copy.wait_recv()
     if n_dp > 1:
@@ -172,6 +157,21 @@
         lax.fori_loop(1, n_ex, send, 0, unroll=n_ex <= 16)
         xrecv[c, mine] = xsend[c, mine]
 
+    lE, lEl, lec = log2(E), log2(E_loc), log2(ec)
+
+    for c in range(chunks):
+        def want(r):
+            g = r >> (lTk + lE)
+            j = (r >> lE) & (Tk - 1)
+            e = r & (E - 1)
+            el = e & (ec - 1)
+            return (e >> lEl) * R + (el * G + g) * Tk + j
+
+        perm_recv[c] = matrix_of(
+            G * Tk * E, n_ex * R, want,
+            lambda r: ((r & (E_loc - 1)) >> lec) == c,
+        )
+
     total = None
     for c in range(chunks):
         most = xrecv.at[c, pl.ds(0, (n_ex - 1) * R)]
@@ -224,7 +224,7 @@
     T = Tl * n_dp
     Tk = T // n_ex
     Fk = D // n_dp
-    ec = 1 if Tk * (Fk // 128) >= 16 else E_loc
+    ec = E_loc
     G = max(1, 16 // (Tk * ec))
     L = Fk // G
     R = ec * G * Tk

time: 28.3 us -> 27.7 us (0.979)
  Pallas kernels: 26.7 us -> 26.1 us
    pallas_call x1, Pallas kernels: 26.7 us -> 26.1 us  [shards(): pl.pallas_call(functools.partial(kernel, cfg), out_shape=jax.ShapeDtypeSt...]
where the time goes in v3:
time: 27.7 us; the launch traced here: 27.6 us
  Pallas kernels  26.1 us (94%)
  local copies, waits for them, and re-layouts  1.47 us (5%)
    pallas_call x1, Pallas kernels, shards(): pl.pallas_call(functools.partial(kernel, cfg), out_shape=jax.ShapeDtypeSt...  26.1 us
    unnamed x1, local copies, waits for them, and re-layouts  1.47 us

profile of v3, /device:TPU:0, one launch (start us, length us, event | category | flops | bytes accessed | tf_op | source)
XLA Modules:
  0.0 27.6 jit_solution(14485108807182738035)
XLA Ops:
  0.0 26.1 %shard_map.46 = f32[4,32,32]{2,1,0:T(8,128)} custom-call(bf16[32,2048]{1,0:T(8,128)(2,1)} %tok_hbm.1, bf16[2,384,2048]{2,1,0:T(8,128)(2,1)} %wg_hbm.1, bf16[2,384,2048]{2,1,0:T(8,128)(2,1)} %wu_hbm.1, bf16[2,384,2048]{2,1,0:T(8,128)(2,1)} %wd_hbm.1), custom_call_target="tpu_custom_call" | custom-call | flops 603979776 | bytes 9437184 | tf_op jit(solution)/shard_map/pallas_call | solution.py:236
  26.1 1.5 %copy.6 = f32[4,32,32]{2,1,0:T(8,128)} copy(f32[4,32,32]{2,1,0:T(8,128)} %shard_map.46) | data formatting | bytes 32768

commit v4 on v3

--- a/solution.py
+++ b/solution.py
@@ -103,13 +103,14 @@
             own[e, lax.rem(dp + n_dp - k, n_dp)] = part[n * Tl:(n + 1) * Tl]
 
     own_tok.wait()
+    first = []
     for e in range(E_loc):
         loads[e, 0].wait()
         loads[e, 1].wait()
         hidden = hidden_of(tok[0], e)
         loads[e, 2].wait()
         project_theirs(hidden, e, (0,))
-        project_mine(hidden, e, (0,))
+        first.append(hidden)
 
     GE = ec * G
     rows = GE * T
@@ -120,13 +121,15 @@
     )
     for copy in tok_copies:
         copy.wait_recv()
-    if n_dp > 1:
-        hidden = []
-        for e in range(E_loc):
-            hidden.append(hidden_of(tok[1:].reshape(T - Tl, D), e))
-            project_theirs(hidden[e], e, range(1, n_dp))
-        for e in range(E_loc):
-            project_mine(hidden[e], e, range(1, n_dp))
+    both = []
+    for e in range(E_loc):
+        both.append(first[e])
+        if n_dp > 1:
+            rest = hidden_of(tok[1:].reshape(T - Tl, D), e)
+            project_theirs(rest, e, range(1, n_dp))
+            both[e] = jnp.concatenate([first[e], rest], axis=0)
+    for e in range(E_loc):
+        project_mine(both[e], e, range(n_dp))
 
     for c in range(chunks):
         pieces = []

time: 27.7 us -> 27.7 us (level)
  no operation moved by 1% of the time
where the time goes in v4:
time: 27.7 us; the launch traced here: 27.5 us
  Pallas kernels  26 us (94%)
  local copies, waits for them, and re-layouts  1.47 us (5%)
    pallas_call x1, Pallas kernels, shards(): pl.pallas_call(functools.partial(kernel, cfg), out_shape=jax.ShapeDtypeSt...  26 us
    unnamed x1, local copies, waits for them, and re-layouts  1.47 us

profile of v4, /device:TPU:0, one launch (start us, length us, event | category | flops | bytes accessed | tf_op | source)
XLA Modules:
  0.0 27.5 jit_solution(10003902869112539230)
XLA Ops:
  0.0 26.0 %shard_map.46 = f32[4,32,32]{2,1,0:T(8,128)} custom-call(bf16[32,2048]{1,0:T(8,128)(2,1)} %tok_hbm.1, bf16[2,384,2048]{2,1,0:T(8,128)(2,1)} %wg_hbm.1, bf16[2,384,2048]{2,1,0:T(8,128)(2,1)} %wu_hbm.1, bf16[2,384,2048]{2,1,0:T(8,128)(2,1)} %wd_hbm.1), custom_call_target="tpu_custom_call" | custom-call | flops 603979776 | bytes 9437184 | tf_op jit(solution)/shard_map/pallas_call | solution.py:239
  26.0 1.5 %copy.6 = f32[4,32,32]{2,1,0:T(8,128)} copy(f32[4,32,32]{2,1,0:T(8,128)} %shard_map.46) | data formatting | bytes 32768
